TPU v7x, 256 devices: a whole 4x4x8 slice. The times are simulated.
256 devices in a mesh: variant: 8 (over x, core), mesh: 32 (over z, y).
Axes of the slice: x: 4, y: 4, z: 8, core: 2. Of those that a mesh axis runs over, the one named last changes fastest.
Arguments:
- snapshots: float32 [8, 64, 524288], P('variant', None, 'mesh'), may hold values from -12 to 12, as said below
- ref_index: int32 [1], replicated, may hold values from 0 to 7
- weight_codes: int32 [8], replicated, may hold values from 1 to 16
Outputs:
- new_basis: float32 [64, 524288], P(None, 'mesh')
Inputs may be any that keep to these rules, and one draw needn't show every extreme that they name: `snapshots`: each variant's snapshot matrix has full rank 64, and the principal angles between any two variants' spans have tangents below 0.8.
All inputs are finite; a program needn't handle non-finite values.
Results may differ from a plain program's by a relative error of at most 0.0001.
Values sent between devices are 32-bit elements; how exact they have to be, the bound alone decides.
A program may use at most 64 MiB of HBM per device.

v0:
```python
import math
import jax
import jax.numpy as jnp
from jax import lax
from jax.sharding import Mesh
from jax.sharding import PartitionSpec as P

VARIANT = ("variant_0", "variant_1")
highest = lax.Precision.HIGHEST
atan_coeffs = [(-1.0) ** k / (2 * k + 1) for k in range(24)]
cos_coeffs = [(-1.0) ** k / math.factorial(2 * k) for k in range(24)]
sin_coeffs = [(-1.0) ** k / math.factorial(2 * k + 1) for k in range(24)]


def from_everyone(x, axis):
    count = lax.axis_size(axis)
    return lax.all_to_all(jnp.broadcast_to(x[None], (count, *x.shape)), axis, 0, 0, tiled=True)


def of_everyone(x, axis):
    everything = from_everyone(x, axis)
    return jnp.sum(everything, axis=0)


def spread(x, axes, root):
    x = jnp.where(lax.axis_index(axes) == root, x, jnp.zeros_like(x))
    for axis in axes:
        x = lax.psum(x, axis)
    return x


def product(left, right):
    return jnp.dot(left, right, precision=highest, preferred_element_type=jnp.float32)


def series(matrix, coeffs):
    eye = jnp.eye(matrix.shape[0], dtype=jnp.float32)
    total = coeffs[-1] * eye
    for coeff in reversed(coeffs[:-1]):
        total = coeff * eye + product(matrix, total)
    return total


def inverse(matrix):
    factor = jnp.linalg.cholesky(product(matrix.T, matrix))
    return jax.scipy.linalg.cho_solve((factor, True), matrix.T)


def on_device(snapshots, ref_index, weight_codes):
    own_snap = snapshots[0]
    root = ref_index[0]
    codes = weight_codes.astype(jnp.float32)
    weight = codes[lax.axis_index(VARIANT)] / jnp.sum(codes)
    eye = jnp.eye(own_snap.shape[0], dtype=jnp.float32)
    scale = jnp.float32(math.sqrt(own_snap.shape[1] * lax.axis_size("mesh")))
    gram_own = of_everyone(product(own_snap, own_snap.T), "mesh")
    lower_own = jnp.linalg.cholesky(gram_own)
    base_own = jax.scipy.linalg.solve_triangular(lower_own, own_snap, lower=True)
    base_ref = spread(base_own, VARIANT, root)
    correlation = of_everyone(product(base_ref, base_own.T), "mesh")
    minv = inverse(correlation)
    tangent = product(minv.T, base_own) - base_ref
    tangent_gram = product(minv.T, minv) - eye
    term = weight * product(series(tangent_gram, atan_coeffs), tangent)
    blended = lax.psum(term, VARIANT)
    energy = of_everyone(product(blended, blended.T), "mesh")
    mixed = product(series(energy, cos_coeffs), base_ref) + product(
        series(energy, sin_coeffs), blended
    )
    return mixed * scale


def solution(mesh):
    finer = Mesh(mesh.devices.reshape(4, 2, mesh.shape["mesh"]), ("variant_0", "variant_1", "mesh"))
    placed = (P(VARIANT, None, "mesh"), P(), P())
    return jax.shard_map(
        on_device, mesh=finer, in_specs=placed, out_specs=P(None, "mesh"), check_vma=False
    )
```

profile of v0, /device:TPU:7, one launch (start us, length us, event | category | flops | bytes accessed | tf_op | source)
XLA Modules:
  0.0 408.7 jit_solution(8007824990110213597)
XLA Ops:
  6.5 6.9 %fusion.3 = f32[64,64]{1,0:T(8,128)S(1)} fusion(f32[1,64,16384]{2,1,0:T(8,128)} %param.4), kind=kOutput, calls=%fused_computation.6 | convolution fusion | flops 805306368 | bytes 4210688 | tf_op jit(solution)/shard_map/dot_general | solution.py:33
  13.6 1.4 reshape.19
  15.0 11.2 %all-to-all-start = ((f32[32,1,4096]{2,1,0:T(1,128)}), f32[32,1,4096]{2,1,0:T(1,128)S(1)}, u32[]{:S(2)}, u32[]{:S(2)}) async-start(f32[32,1,4096]{2,1,0:T(1,128)} %reshape.19), calls=%async_computation | async-start | bytes 1048576 | tf_op jit(solution)/shard_map/all_to_all | solution.py:17
  27.3 15.3 %all-to-all-done = f32[32,1,4096]{2,1,0:T(1,128)S(1)} async-done(((f32[32,1,4096]{2,1,0:T(1,128)}), f32[32,1,4096]{2,1,0:T(1,128)S(1)}, u32[]{:S(2)}, u32[]{:S(2)}) %all-to-all-start) | async-done | bytes 524320 | tf_op jit(solution)/shard_map/all_to_all | solution.py:17
  43.1 1.9 reduce.4
  45.5 5.8 %cholesky.44 = f32[64,64]{1,0:T(8,128)S(1)} custom-call(f32[64,64]{1,0:T(8,128)S(1)} %fusion.15), custom_call_target="Cholesky" | custom-call | tf_op jit(solution)/shard_map/jit(cholesky)/cholesky | solution.py:57
  51.4 0.6 compare_reduce_fusion.1
  52.1 0.7 fusion.7
  52.7 4.9 %custom-call.13 = f32[1,64,64]{1,2,0:T(8,128)S(1)} custom-call(f32[1,64,64]{2,1,0:T(8,128)S(1)} %fusion.7), custom_call_target="InvertDiagBlocksLowerTriangular" | custom-call | tf_op jit(solution)/shard_map/jit(_solve_triangular)/triangular_solve | solution.py:58
  57.6 9.3 %broadcast_select_fusion = (f32[64,16384]{1,0:T(8,128)}, f32[64,16384]{1,0:T(8,128)}) fusion(pred[]{:T(512)S(6)} %eq.142, f32[1,64,16384]{2,1,0:T(8,128)} %param.4, f32[1,64,64]{1,2,0:T(8,128)S(1)} %custom-call.13), kind=kOutput, calls=%fused_computation.8 | convolution fusion | flops 806354944 | bytes 12599297 | tf_op jit(solution)/shard_map/jit(_solve_triangular)/triangular_solve | solution.py:58
  67.0 94.0 %all-reduce.4.cloned.1.call-done = f32[64,16384]{1,0:T(8,128)} async-done(((f32[64,16384]{1,0:T(8,128)}), f32[64,16384]{1,0:T(8,128)}) %all-reduce.4.cloned.1.call-update) | async-done | bytes 4194320 | tf_op jit(solution)/shard_map/psum | solution.py:28
  161.0 44.4 %all-reduce.6.cloned.1.call-done = f32[64,16384]{1,0:T(8,128)} async-done(((f32[64,16384]{1,0:T(8,128)}), f32[64,16384]{1,0:T(8,128)}) %all-reduce.6.cloned.1.call-update) | async-done | bytes 4194320 | tf_op jit(solution)/shard_map/psum | solution.py:28
  205.4 6.9 %fusion.35 = f32[64,64]{1,0:T(8,128)S(1)} fusion(f32[64,16384]{1,0:T(8,128)} %all-reduce.6.cloned.1.call-done, f32[64,16384]{1,0:T(8,128)} %get-tuple-element.7), kind=kOutput, calls=%fused_computation.114 | convolution fusion | flops 805306368 | bytes 8404992 | tf_op jit(solution)/shard_map/dot_general | solution.py:33
  212.5 1.4 reshape.21
  213.9 9.6 %all-to-all-start.1 = ((f32[32,1,4096]{2,1,0:T(1,128)}), f32[32,1,4096]{2,1,0:T(1,128)S(1)}, u32[]{:S(2)}, u32[]{:S(2)}) async-start(f32[32,1,4096]{2,1,0:T(1,128)} %reshape.21), calls=%async_computation.1 | async-start | bytes 1048576 | tf_op jit(solution)/shard_map/all_to_all | solution.py:17
  223.6 0.6 dynamic_slice.3
  224.1 0.6 convert_reduce_fusion
  226.0 14.2 %all-to-all-done.1 = f32[32,1,4096]{2,1,0:T(1,128)S(1)} async-done(((f32[32,1,4096]{2,1,0:T(1,128)}), f32[32,1,4096]{2,1,0:T(1,128)S(1)}, u32[]{:S(2)}, u32[]{:S(2)}) %all-to-all-start.1) | async-done | bytes 524320 | tf_op jit(solution)/shard_map/all_to_all | solution.py:17
  240.2 1.9 reduce.5
  242.9 5.8 %cholesky.55 = f32[64,64]{1,0:T(8,128)S(1)} custom-call(f32[64,64]{1,0:T(8,128)S(1)} %fusion.13), custom_call_target="Cholesky" | custom-call | tf_op jit(solution)/shard_map/jit(cholesky)/cholesky | solution.py:45
  248.8 0.6 compare_reduce_fusion
  249.4 0.7 fusion.8
  250.1 4.9 %custom-call.14 = f32[1,64,64]{1,2,0:T(8,128)S(1)} custom-call(f32[1,64,64]{2,1,0:T(8,128)S(1)} %fusion.8), custom_call_target="InvertDiagBlocksLowerTriangular" | custom-call | tf_op jit(solution)/shard_map/jit(_cho_solve)/triangular_solve | solution.py:46
  259.5 7.2 %convolution_subtract_fusion = f32[64,16384]{1,0:T(8,128)S(1)} fusion(f32[64,16384]{1,0:T(8,128)} %all-reduce.6.cloned.1.call-done, f32[64,64]{1,0:T(8,128)S(1)} %fusion.9, f32[64,16384]{1,0:T(8,128)} %get-tuple-element.7), kind=kOutput, calls=%fused_computation.3 | convolution fusion | flops 806354944 | bytes 12599296 | tf_op jit(solution)/shard_map/dot_general | solution.py:33
  266.7 5.4 %convolution_multiply_fusion = f32[64,16384]{1,0:T(8,128)} fusion(f32[64,64]{1,0:T(8,128)S(1)} %convolution_add_fusion.40, f32[64,16384]{1,0:T(8,128)S(1)} %convolution_subtract_fusion, f32[]{:T(128)S(6)} %div.9), kind=kOutput, calls=%fused_computation.2 | convolution fusion | flops 806354944 | bytes 8404996 | tf_op jit(solution)/shard_map/dot_general | solution.py:33
  272.1 74.9 %all-reduce.8.cloned.1.call-done = f32[64,16384]{1,0:T(8,128)} async-done(((f32[64,16384]{1,0:T(8,128)}), f32[64,16384]{1,0:T(8,128)}) %all-reduce.8.cloned.1.call-update) | async-done | bytes 4194320 | tf_op jit(solution)/shard_map/psum | solution.py:65
  347.0 6.9 %fusion.37 = f32[64,64]{1,0:T(8,128)S(1)} fusion(f32[64,16384]{1,0:T(8,128)} %all-reduce.8.cloned.1.call-done), kind=kOutput, calls=%fused_computation.116 | convolution fusion | flops 805306368 | bytes 4210688 | tf_op jit(solution)/shard_map/dot_general | solution.py:33
  354.0 0.7 reshape.23
  354.7 26.7 %all_to_all.15 = f32[32,1,4096]{2,1,0:T(1,128)S(1)} all-to-all(f32[32,1,4096]{2,1,0:T(1,128)S(1)} %reshape.23), channel_id=1, replica_groups=mesh['variant_0'=4,'variant_1'=2,'mesh'=32] {'mesh'}, dimensions={0} | all-to-all | bytes 1048576 | tf_op jit(solution)/shard_map/all_to_all | solution.py:17
  381.4 1.9 reduce.6
  390.9 5.6 %fusion.40 = f32[64,16384]{1,0:T(8,128)S(1)} fusion(f32[64,64]{1,0:T(8,128)S(1)} %convolution_add_fusion.20, f32[64,16384]{1,0:T(8,128)} %all-reduce.6.cloned.1.call-done), kind=kOutput, calls=%fused_computation.119 | convolution fusion | flops 805306368 | bytes 8404992 | tf_op jit(solution)/shard_map/dot_general | solution.py:33
  396.5 5.4 %fusion = f32[64,16384]{1,0:T(8,128)} fusion(f32[64,16384]{1,0:T(8,128)S(1)} %fusion.40, f32[64,64]{1,0:T(8,128)S(1)} %convolution_add_fusion.1, f32[64,16384]{1,0:T(8,128)S(1)} %copy-done), kind=kOutput, calls=%fused_computation.1 | convolution fusion | flops 807403520 | bytes 12599296 | tf_op jit(solution)/shard_map/dot_general | solution.py:33
  (96 shorter events, 14.5 us)
Async XLA Ops:
  15.0 27.5 %all-to-all-start = ((f32[32,1,4096]{2,1,0:T(1,128)}), f32[32,1,4096]{2,1,0:T(1,128)S(1)}, u32[]{:S(2)}, u32[]{:S(2)}) async-start(f32[32,1,4096]{2,1,0:T(1,128)} %reshape.19), calls=%async_computation | async-start | bytes 1048576 | tf_op jit(solution)/shard_map/all_to_all | solution.py:17
  26.3 134.7 %all-reduce.4.cloned.1.call-start = ((), (), s32[]{:S(2)}) async-start(), calls=%async_computation.3 | async-start | bytes 8388608 | tf_op jit(solution)/shard_map/psum | solution.py:28
  66.9 138.5 %all-reduce.6.cloned.1.call-start = ((), (), s32[]{:S(2)}) async-start(), calls=%async_computation.4 | async-start | bytes 8388608 | tf_op jit(solution)/shard_map/psum | solution.py:28
  205.4 18.2 %copy-start.1 = (s32[8]{0:T(128)S(1)}, s32[8]{0:T(128)}, u32[]{:S(2)}) copy-start(s32[8]{0:T(128)} %param.6) | copy-start | bytes 100
  213.9 26.2 %all-to-all-start.1 = ((f32[32,1,4096]{2,1,0:T(1,128)}), f32[32,1,4096]{2,1,0:T(1,128)S(1)}, u32[]{:S(2)}, u32[]{:S(2)}) async-start(f32[32,1,4096]{2,1,0:T(1,128)} %reshape.21), calls=%async_computation.1 | async-start | bytes 1048576 | tf_op jit(solution)/shard_map/all_to_all | solution.py:17
  223.5 123.5 %all-reduce.8.cloned.1.call-start = ((), (), s32[]{:S(2)}) async-start(), calls=%async_computation.5 | async-start | bytes 8388608 | tf_op jit(solution)/shard_map/psum | solution.py:65
  390.9 5.6 %copy-start = (f32[64,16384]{1,0:T(8,128)S(1)}, f32[64,16384]{1,0:T(8,128)}, u32[]{:S(2)}) copy-start(f32[64,16384]{1,0:T(8,128)} %all-reduce.8.cloned.1.call-done) | copy-start | bytes 12582916
Sparse Core Ops, SparseCore 0:
  67.1 93.8 all-reduce.3
  163.9 41.4 all-reduce.5
  272.2 74.6 all-reduce.7
where the time goes:
time: 413 us; the launch traced here: 409 us
  waiting for transfers between devices  243 us (59%)
  matrix products  65.1 us (16%)
  other arithmetic  30.6 us (7%)
  blocking collectives  26.7 us (6%)
  starting transfers between devices  21.2 us (5%)
  between operations  16 us (4%)
  local copies, waits for them, and re-layouts  6.37 us (2%)
    psum x2, waiting for transfers between devices, spread(): x = lax.psum(x, axis)  138 us
    psum x1, waiting for transfers between devices, on_device(): blended = lax.psum(term, VARIANT)  74.9 us
    dot_general x74, matrix products, product(): jnp.dot(left, right, precision=highest, preferred_element_type=jnp.float32)  55.4 us
    all_to_all x2, waiting for transfers between devices, from_everyone(): lax.all_to_all(jnp.broadcast_to(x[None], (count, *x.shape)), axis, 0, 0,...  29.4 us
    all_to_all x1, blocking collectives, from_everyone(): lax.all_to_all(jnp.broadcast_to(x[None], (count, *x.shape)), axis, 0, 0,...  26.7 us
    all_to_all x2, starting transfers between devices, from_everyone(): lax.all_to_all(jnp.broadcast_to(x[None], (count, *x.shape)), axis, 0, 0,...  20.8 us
    another operation x1, matrix products, on_device(): jax.scipy.linalg.solve_triangular(lower_own, own_snap, lower=True)  9.3 us
  transfers between devices with their start and end apart: 5, of which 5 were waited for; matrix products, arithmetic and copies ran while one was open for 0% of the time, Pallas kernels for 0%

commit v1 on v0

--- a/solution.py
+++ b/solution.py
@@ -10,6 +10,10 @@
 atan_coeffs = [(-1.0) ** k / (2 * k + 1) for k in range(24)]
 cos_coeffs = [(-1.0) ** k / math.factorial(2 * k) for k in range(24)]
 sin_coeffs = [(-1.0) ** k / math.factorial(2 * k + 1) for k in range(24)]
+
+
+def check_sector(original):
+    return jax.lax.psum(jax.lax.psum(original, axis_name="variant_0"), axis_name="variant_1")
 
 
 def from_everyone(x, axis):
@@ -62,7 +66,7 @@
     tangent = product(minv.T, base_own) - base_ref
     tangent_gram = product(minv.T, minv) - eye
     term = weight * product(series(tangent_gram, atan_coeffs), tangent)
-    blended = lax.psum(term, VARIANT)
+    blended = check_sector(term)
     energy = of_everyone(product(blended, blended.T), "mesh")
     mixed = product(series(energy, cos_coeffs), base_ref) + product(
         series(energy, sin_coeffs), blended

time: 413 us -> 477 us (1.15)
  waiting for transfers between devices: 243 us -> 305 us
    psum x1 -> x2, waiting for transfers between devices: 74.9 us -> 138 us  [the longest x1 93.4 us: check_sector(): jax.lax.psum(original, axis_name='variant_0')]
  transfers between devices with their start and end apart: 5 -> 6, of which waited for: 5 -> 6; matrix products, arithmetic and copies ran while one was open for 0% -> 0% of each run, Pallas kernels for 0% -> 0%
where the time goes in v1:
time: 477 us; the launch traced here: 471 us
  waiting for transfers between devices  305 us (64%)
  matrix products  64.9 us (14%)
  other arithmetic  30.6 us (6%)
  blocking collectives  26 us (5%)
  starting transfers between devices  21.6 us (5%)
  between operations  16 us (3%)
  local copies, waits for them, and re-layouts  6.37 us (1%)
    psum x2, waiting for transfers between devices, spread(): x = lax.psum(x, axis)  138 us
    psum x1, waiting for transfers between devices, check_sector(): jax.lax.psum(original, axis_name='variant_0')  93.4 us
    dot_general x74, matrix products, product(): jnp.dot(left, right, precision=highest, preferred_element_type=jnp.float32)  55.2 us
    psum x1, waiting for transfers between devices, check_sector(): jax.lax.psum(jax.lax.psum(original, axis_name='variant_0'), axis_name='va...  44.3 us
    all_to_all x2, waiting for transfers between devices, from_everyone(): lax.all_to_all(jnp.broadcast_to(x[None], (count, *x.shape)), axis, 0, 0,...  29.3 us
    all_to_all x1, blocking collectives, from_everyone(): lax.all_to_all(jnp.broadcast_to(x[None], (count, *x.shape)), axis, 0, 0,...  26 us
    all_to_all x2, starting transfers between devices, from_everyone(): lax.all_to_all(jnp.broadcast_to(x[None], (count, *x.shape)), axis, 0, 0,...  20.8 us
  transfers between devices with their start and end apart: 6, of which 6 were waited for; matrix products, arithmetic and copies ran while one was open for 0% of the time, Pallas kernels for 0%

profile of v1, /device:TPU:7, one launch (start us, length us, event | category | flops | bytes accessed | tf_op | source)
XLA Modules:
  0.0 470.9 jit_solution(15399729933870020874)
XLA Ops:
  6.5 6.9 %fusion.3 = f32[64,64]{1,0:T(8,128)S(1)} fusion(f32[1,64,16384]{2,1,0:T(8,128)} %param.4), kind=kOutput, calls=%fused_computation.6 | convolution fusion | flops 805306368 | bytes 4210688 | tf_op jit(solution)/shard_map/dot_general | solution.py:37
  13.6 1.4 reshape.19
  15.0 11.2 %all-to-all-start = ((f32[32,1,4096]{2,1,0:T(1,128)}), f32[32,1,4096]{2,1,0:T(1,128)S(1)}, u32[]{:S(2)}, u32[]{:S(2)}) async-start(f32[32,1,4096]{2,1,0:T(1,128)} %reshape.19), calls=%async_computation | async-start | bytes 1048576 | tf_op jit(solution)/shard_map/all_to_all | solution.py:21
  27.4 15.1 %all-to-all-done = f32[32,1,4096]{2,1,0:T(1,128)S(1)} async-done(((f32[32,1,4096]{2,1,0:T(1,128)}), f32[32,1,4096]{2,1,0:T(1,128)S(1)}, u32[]{:S(2)}, u32[]{:S(2)}) %all-to-all-start) | async-done | bytes 524320 | tf_op jit(solution)/shard_map/all_to_all | solution.py:21
  43.1 1.9 reduce.4
  45.5 5.8 %cholesky.44 = f32[64,64]{1,0:T(8,128)S(1)} custom-call(f32[64,64]{1,0:T(8,128)S(1)} %fusion.15), custom_call_target="Cholesky" | custom-call | tf_op jit(solution)/shard_map/jit(cholesky)/cholesky | solution.py:61
  51.4 0.6 compare_reduce_fusion.1
  52.1 0.7 fusion.7
  52.7 4.9 %custom-call.13 = f32[1,64,64]{1,2,0:T(8,128)S(1)} custom-call(f32[1,64,64]{2,1,0:T(8,128)S(1)} %fusion.7), custom_call_target="InvertDiagBlocksLowerTriangular" | custom-call | tf_op jit(solution)/shard_map/jit(_solve_triangular)/triangular_solve | solution.py:62
  57.6 9.3 %broadcast_select_fusion = (f32[64,16384]{1,0:T(8,128)}, f32[64,16384]{1,0:T(8,128)}) fusion(pred[]{:T(512)S(6)} %eq.142, f32[1,64,16384]{2,1,0:T(8,128)} %param.4, f32[1,64,64]{1,2,0:T(8,128)S(1)} %custom-call.13), kind=kOutput, calls=%fused_computation.8 | convolution fusion | flops 806354944 | bytes 12599297 | tf_op jit(solution)/shard_map/jit(_solve_triangular)/triangular_solve | solution.py:62
  67.0 94.0 %all-reduce.5.cloned.1.call-done = f32[64,16384]{1,0:T(8,128)} async-done(((f32[64,16384]{1,0:T(8,128)}), f32[64,16384]{1,0:T(8,128)}) %all-reduce.5.cloned.1.call-update) | async-done | bytes 4194320 | tf_op jit(solution)/shard_map/psum | solution.py:32
  161.0 44.4 %all-reduce.7.cloned.1.call-done = f32[64,16384]{1,0:T(8,128)} async-done(((f32[64,16384]{1,0:T(8,128)}), f32[64,16384]{1,0:T(8,128)}) %all-reduce.7.cloned.1.call-update) | async-done | bytes 4194320 | tf_op jit(solution)/shard_map/psum | solution.py:32
  205.4 6.9 %fusion.35 = f32[64,64]{1,0:T(8,128)S(1)} fusion(f32[64,16384]{1,0:T(8,128)} %all-reduce.7.cloned.1.call-done, f32[64,16384]{1,0:T(8,128)} %get-tuple-element.7), kind=kOutput, calls=%fused_computation.114 | convolution fusion | flops 805306368 | bytes 8404992 | tf_op jit(solution)/shard_map/dot_general | solution.py:37
  212.5 1.4 reshape.21
  213.9 9.6 %all-to-all-start.1 = ((f32[32,1,4096]{2,1,0:T(1,128)}), f32[32,1,4096]{2,1,0:T(1,128)S(1)}, u32[]{:S(2)}, u32[]{:S(2)}) async-start(f32[32,1,4096]{2,1,0:T(1,128)} %reshape.21), calls=%async_computation.1 | async-start | bytes 1048576 | tf_op jit(solution)/shard_map/all_to_all | solution.py:21
  224.1 0.6 convert_reduce_fusion
  226.0 14.2 %all-to-all-done.1 = f32[32,1,4096]{2,1,0:T(1,128)S(1)} async-done(((f32[32,1,4096]{2,1,0:T(1,128)}), f32[32,1,4096]{2,1,0:T(1,128)S(1)}, u32[]{:S(2)}, u32[]{:S(2)}) %all-to-all-start.1) | async-done | bytes 524320 | tf_op jit(solution)/shard_map/all_to_all | solution.py:21
  240.2 1.9 reduce.5
  242.9 5.8 %cholesky.55 = f32[64,64]{1,0:T(8,128)S(1)} custom-call(f32[64,64]{1,0:T(8,128)S(1)} %fusion.13), custom_call_target="Cholesky" | custom-call | tf_op jit(solution)/shard_map/jit(cholesky)/cholesky | solution.py:49
  248.8 0.6 compare_reduce_fusion
  249.4 0.7 fusion.8
  250.1 4.9 %custom-call.14 = f32[1,64,64]{1,2,0:T(8,128)S(1)} custom-call(f32[1,64,64]{2,1,0:T(8,128)S(1)} %fusion.8), custom_call_target="InvertDiagBlocksLowerTriangular" | custom-call | tf_op jit(solution)/shard_map/jit(_cho_solve)/triangular_solve | solution.py:50
  259.5 7.2 %convolution_subtract_fusion = f32[64,16384]{1,0:T(8,128)S(1)} fusion(f32[64,16384]{1,0:T(8,128)} %all-reduce.7.cloned.1.call-done, f32[64,64]{1,0:T(8,128)S(1)} %fusion.9, f32[64,16384]{1,0:T(8,128)} %get-tuple-element.7), kind=kOutput, calls=%fused_computation.3 | convolution fusion | flops 806354944 | bytes 12599296 | tf_op jit(solution)/shard_map/dot_general | solution.py:37
  266.7 5.2 %convolution_multiply_fusion = f32[64,16384]{1,0:T(8,128)} fusion(f32[64,64]{1,0:T(8,128)S(1)} %convolution_add_fusion.40, f32[64,16384]{1,0:T(8,128)S(1)} %convolution_subtract_fusion, f32[]{:T(128)S(6)} %div.9), kind=kOutput, calls=%fused_computation.2 | convolution fusion | flops 806354944 | bytes 8404996 | tf_op jit(solution)/shard_map/dot_general | solution.py:37
  272.2 93.4 %all-reduce.9.cloned.1.call-done = f32[64,16384]{1,0:T(8,128)} async-done(((f32[64,16384]{1,0:T(8,128)}), f32[64,16384]{1,0:T(8,128)}) %all-reduce.9.cloned.1.call-update) | async-done | bytes 4194320 | tf_op jit(solution)/shard_map/psum | solution.py:16
  365.6 44.3 %all-reduce.11.cloned.1.call-done = f32[64,16384]{1,0:T(8,128)} async-done(((f32[64,16384]{1,0:T(8,128)}), f32[64,16384]{1,0:T(8,128)}) %all-reduce.11.cloned.1.call-update) | async-done | bytes 4194320 | tf_op jit(solution)/shard_map/psum | solution.py:16
  409.9 6.9 %fusion.37 = f32[64,64]{1,0:T(8,128)S(1)} fusion(f32[64,16384]{1,0:T(8,128)} %all-reduce.11.cloned.1.call-done), kind=kOutput, calls=%fused_computation.116 | convolution fusion | flops 805306368 | bytes 4210688 | tf_op jit(solution)/shard_map/dot_general | solution.py:37
  417.0 0.7 reshape.23
  417.6 26.0 %all_to_all.15 = f32[32,1,4096]{2,1,0:T(1,128)S(1)} all-to-all(f32[32,1,4096]{2,1,0:T(1,128)S(1)} %reshape.23), channel_id=1, replica_groups=mesh['variant_0'=4,'variant_1'=2,'mesh'=32] {'mesh'}, dimensions={0} | all-to-all | bytes 1048576 | tf_op jit(solution)/shard_map/all_to_all | solution.py:21
  443.6 1.9 reduce.6
  453.2 5.6 %fusion.40 = f32[64,16384]{1,0:T(8,128)S(1)} fusion(f32[64,64]{1,0:T(8,128)S(1)} %convolution_add_fusion.20, f32[64,16384]{1,0:T(8,128)} %all-reduce.7.cloned.1.call-done), kind=kOutput, calls=%fused_computation.119 | convolution fusion | flops 805306368 | bytes 8404992 | tf_op jit(solution)/shard_map/dot_general | solution.py:37
  458.8 5.4 %fusion = f32[64,16384]{1,0:T(8,128)} fusion(f32[64,16384]{1,0:T(8,128)S(1)} %fusion.40, f32[64,64]{1,0:T(8,128)S(1)} %convolution_add_fusion.1, f32[64,16384]{1,0:T(8,128)S(1)} %copy-done), kind=kOutput, calls=%fused_computation.1 | convolution fusion | flops 807403520 | bytes 12599296 | tf_op jit(solution)/shard_map/dot_general | solution.py:37
  (99 shorter events, 15.5 us)
Async XLA Ops:
  15.0 27.5 %all-to-all-start = ((f32[32,1,4096]{2,1,0:T(1,128)}), f32[32,1,4096]{2,1,0:T(1,128)S(1)}, u32[]{:S(2)}, u32[]{:S(2)}) async-start(f32[32,1,4096]{2,1,0:T(1,128)} %reshape.19), calls=%async_computation | async-start | bytes 1048576 | tf_op jit(solution)/shard_map/all_to_all | solution.py:21
  26.3 134.7 %all-reduce.5.cloned.1.call-start = ((), (), s32[]{:S(2)}) async-start(), calls=%async_computation.3 | async-start | bytes 8388608 | tf_op jit(solution)/shard_map/psum | solution.py:32
  66.9 138.5 %all-reduce.7.cloned.1.call-start = ((), (), s32[]{:S(2)}) async-start(), calls=%async_computation.4 | async-start | bytes 8388608 | tf_op jit(solution)/shard_map/psum | solution.py:32
  205.4 18.2 %copy-start.1 = (s32[8]{0:T(128)S(1)}, s32[8]{0:T(128)}, u32[]{:S(2)}) copy-start(s32[8]{0:T(128)} %param.6) | copy-start | bytes 100
  213.9 26.2 %all-to-all-start.1 = ((f32[32,1,4096]{2,1,0:T(1,128)}), f32[32,1,4096]{2,1,0:T(1,128)S(1)}, u32[]{:S(2)}, u32[]{:S(2)}) async-start(f32[32,1,4096]{2,1,0:T(1,128)} %reshape.21), calls=%async_computation.1 | async-start | bytes 1048576 | tf_op jit(solution)/shard_map/all_to_all | solution.py:21
  223.5 142.1 %all-reduce.9.cloned.1.call-start = ((), (), s32[]{:S(2)}) async-start(), calls=%async_computation.5 | async-start | bytes 8388608 | tf_op jit(solution)/shard_map/psum | solution.py:16
  272.0 137.9 %all-reduce.11.cloned.1.call-start = ((), (), s32[]{:S(2)}) async-start(), calls=%async_computation.6 | async-start | bytes 8388608 | tf_op jit(solution)/shard_map/psum | solution.py:16
  453.2 5.6 %copy-start = (f32[64,16384]{1,0:T(8,128)S(1)}, f32[64,16384]{1,0:T(8,128)}, u32[]{:S(2)}) copy-start(f32[64,16384]{1,0:T(8,128)} %all-reduce.11.cloned.1.call-done) | copy-start | bytes 12582916
Sparse Core Ops, SparseCore 0:
  67.1 93.8 all-reduce.4
  163.9 41.4 all-reduce.6
  272.1 93.4 all-reduce.8
  368.4 41.4 all-reduce.10
